TPU v7x, 1024 devices: a whole 8x8x8 slice. The times are simulated.
1024 devices in a mesh: inner: 16 (over z_hi, x), outer: 64 (over z_lo, y, core).
Axes of the slice: x: 8, y: 8, z: 8 (z_hi: 2, z_lo: 4; z = z_hi * 4 + z_lo), core: 2. Of those that a mesh axis runs over, the one named last changes fastest.
Arguments:
- activations: bfloat16 [131072, 8192], P(('inner', 'outer')), may hold values from -6 to 6
- cotangent: bfloat16 [131072, 256], P(('inner', 'outer')), may hold values from -6 to 6
- token_ids: int32 [131072], P(('inner', 'outer')), may hold values from 0 to 128255, as said below
- kept_rows: int32 [2, 32], replicated, may hold values from 0 to 63, as said below
Outputs:
- grad_blocks: float32 [8192, 128], P(('inner', 'outer'))
Inputs may be any that keep to these rules, and one draw needn't show every extreme that they name: `token_ids`: in each of the runs of 128 tokens that one device holds, the last 1 to 64 tokens are padding with id 0 and no other token has id 0. `kept_rows`: each row lists 32 distinct block rows in increasing order.
All inputs are finite; a program needn't handle non-finite values.
Results may differ from a plain program's by a relative error of at most 0.0003.
Values sent between devices are 32-bit elements; how exact they have to be, the bound alone decides.
No kernel may reach another device: no remote copies, remote signals or barrier semaphores. Data moves between devices by JAX's collectives and lax.ppermute only.
A program may use at most 32 MiB of HBM per device.

v0:
```python
import math

import jax
import jax.numpy as jnp
from jax import lax
from jax.sharding import PartitionSpec as P


def local(activations, cotangent, token_ids, kept_rows):
    tok_rows = activations.shape[0]
    feat_width = activations.shape[1]
    columns = kept_rows.shape[0]
    kept_count = kept_rows.shape[1]
    block_size = feat_width // (2 * kept_count)
    live_grad = jnp.where((token_ids != 0)[:, None], cotangent, jnp.zeros_like(cotangent))
    blocks_view = activations.reshape(tok_rows, feat_width // block_size, block_size)
    picked = jnp.take(blocks_view, kept_rows.reshape(-1), axis=1)
    picked = picked.reshape(tok_rows, columns, kept_count, block_size)
    targets = live_grad.reshape(tok_rows, columns, block_size)
    partial_term = jnp.einsum("tjki,tjc->jkic", picked, targets, preferred_element_type=jnp.float32)
    partial_term = partial_term.reshape(columns * kept_count * block_size, block_size)
    inner_size = lax.axis_size("inner")
    outer_size = lax.axis_size("outer")
    group_sum = lax.psum_scatter(partial_term, "inner", scatter_dimension=0, tiled=True)
    summed = lax.psum_scatter(group_sum, "outer", scatter_dimension=0, tiled=True)
    grad_scale = 1.0 / math.sqrt(tok_rows * inner_size * outer_size)
    return summed * jnp.float32(grad_scale)


def solution(mesh):
    in_specs = (
        P(("inner", "outer"), None),
        P(("inner", "outer"), None),
        P(("inner", "outer")),
        P(),
    )
    out_specs = P(("inner", "outer"), None)
    return jax.shard_map(local, mesh=mesh, in_specs=in_specs, out_specs=out_specs, check_vma=False)
```

profile of v0, /device:TPU:1, one launch (start us, length us, event | category | flops | bytes accessed | tf_op | source)
XLA Modules:
  0.0 788.0 jit_solution(15456217225029758400)
XLA Ops:
  6.5 0.0 reduce-scatter.2.cloned.1.call-start
  6.5 0.8 reshape.51
  7.3 0.7 compare_and_fusion
  8.0 4.1 copy.13
  12.1 3.2 copy.14
  15.3 2.2 gather_fusion
  17.5 0.0 copy-start.1
  17.5 0.0 copy-start
  17.5 3.2 copy.15
  20.6 0.0 copy-done.1
  20.7 0.0 copy-done
  20.7 0.1 broadcast_select_fusion
  20.8 2.7 fusion
  23.5 0.0 reduce-scatter.2.cloned.1.call-update
  23.5 0.0 all-reduce.3.cloned.1.call-start
  23.6 254.6 %reduce-scatter.2.cloned.1.call-done = f32[512,128]{1,0:T(8,128)} async-done(((f32[8192,128]{1,0:T(8,128)}), f32[512,128]{1,0:T(8,128)}) %reduce-scatter.2.cloned.1.call-update) | async-done | bytes 262160 | tf_op jit(solution)/shard_map/reduce_scatter | solution.py:24
  278.2 0.0 all-reduce.3.cloned.1.call-update
  278.2 1.3 dynamic-slice
  280.1 499.8 %all-reduce.3.cloned.1.call-done = f32[512,128]{1,0:T(8,128)} async-done(((f32[512,128]{1,0:T(8,128)}), f32[512,128]{1,0:T(8,128)}) %all-reduce.3.cloned.1.call-update) | async-done | bytes 262160
  779.9 1.3 dynamic-slice_multiply_fusion
  (4 shorter events, 0.0 us)
Async XLA Ops:
  6.5 271.6 %reduce-scatter.2.cloned.1.call-start = ((), (), s32[]{:S(2)}) async-start(), calls=%async_computation.1 | async-start | bytes 4456448 | tf_op jit(solution)/shard_map/reduce_scatter | solution.py:24
  17.5 3.2 copy-start.1
  17.5 3.2 copy-start
  23.5 756.4 %all-reduce.3.cloned.1.call-start = ((), (), s32[]{:S(2)}) async-start(), calls=%async_computation.2 | async-start | bytes 524288
Sparse Core Ops, SparseCore 0:
  23.6 254.5 reduce-scatter.1
  281.7 498.2 all-reduce.2
where the time goes:
time: 788 us
  waiting for transfers between devices  754 us (96%)
  local copies, waits for them, and re-layouts  14.7 us (2%)
  between operations  14.1 us (2%)
    unnamed x3, waiting for transfers between devices  500 us
    reduce_scatter x1, waiting for transfers between devices, local(): lax.psum_scatter(partial_term, 'inner', scatter_dimension=0, tiled=True)  255 us
  transfers between devices with their start and end apart: 2, of which 2 were waited for; matrix products, arithmetic and copies ran while one was open for 0% of the time, Pallas kernels for 0%

commit v1 on v0

v1 whole, which is shorter than its diff:
```python
import math

import jax
import jax.numpy as jnp
import numpy as np
from jax import lax
from jax.experimental import pallas as pl
from jax.experimental.pallas import tpu as pltpu
from jax.sharding import Mesh, PartitionSpec as P

ZH, X, ZL, Y, C = 2, 8, 4, 8, 2
Z = ZH * ZL
ALL = ZH * X * ZL * Y * C
ROWS = 8


def number(x, y, z, c):
    return (((z // ZL * X + x) * ZL + z % ZL) * Y + y) * C + c


def line(axis, x, y, z, c):
    if axis == "x":
        return [number(i, y, z, c) for i in range(X)]
    if axis == "y":
        return [number(x, i, z, c) for i in range(Y)]
    return [number(x, y, i, c) for i in range(Z)]


def lines(axis_of_core):
    groups = {
        tuple(line(axis_of_core[c], x, y, z, c))
        for x in range(X)
        for y in range(Y)
        for z in range(Z)
        for c in range(C)
    }
    return [list(g) for g in sorted(groups)]


def products(kept_ref, ids_ref, grad_ref, act_ref, mine_ref, send_ref):
    core = lax.rem(lax.axis_index("d"), C)
    width = ids_ref.shape[1]
    live = jnp.transpose(jnp.broadcast_to(ids_ref[...], (width, width))) != 0
    targets = [
        jnp.where(live, grad_ref[:, j * width:(j + 1) * width].astype(jnp.float32), 0.0).astype(jnp.bfloat16)
        for j in range(ZH)
    ]

    def run(own):
        zero_ref, one_ref = (mine_ref, send_ref) if own == 0 else (send_ref, mine_ref)

        def step(k, carry):
            x, zl = k // ZL, lax.rem(k, ZL)
            for j in range(ZH):
                z = j * ZL + zl
                start = pl.multiple_of(kept_ref[j, k] * width, width)
                block = act_ref[:, pl.ds(start, width)]
                sums = lax.dot_general(
                    block, targets[j], (((0,), (0,)), ((), ())), preferred_element_type=jnp.float32
                ).reshape(Y, C, ROWS, width)
                zero_ref[x, :, z] = sums[:, 0]
                one_ref[:, z, x] = sums[:, 1]
            return carry

        lax.fori_loop(0, X * ZL, step, 0, unroll=4)

    pl.when(core == 0)(lambda: run(0))
    pl.when(core == 1)(lambda: run(1))


def local(activations, cotangent, token_ids, kept_rows):
    tokens = activations.shape[0]
    tile = (ROWS, tokens)
    vmem = pl.BlockSpec(memory_space=pltpu.VMEM)
    mine, send = pl.pallas_call(
        products,
        out_shape=[jax.ShapeDtypeStruct((8, 8, 8) + tile, jnp.float32)] * 2,
        in_specs=[pl.BlockSpec(memory_space=pltpu.SMEM), vmem, vmem, vmem],
        out_specs=[vmem, vmem],
        compiler_params=pltpu.CompilerParams(vmem_limit_bytes=48 * 1024 * 1024),
        name="products",
    )(kept_rows, token_ids.reshape(1, tokens), cotangent, activations)
    other = lax.ppermute(send, "d", [(i, i ^ 1) for i in range(ALL)])
    held = mine + other
    for axes in (("x", "y"), ("y", "z"), ("z", "x")):
        parts = lax.all_to_all(
            held, "d", split_axis=0, concat_axis=0, axis_index_groups=lines(axes), tiled=True
        )
        held = jnp.sum(parts, axis=0)
    return held * jnp.float32(1.0 / math.sqrt(tokens * ALL))


def solution(mesh):
    flat = Mesh(np.asarray(mesh.devices).reshape(-1), ("d",))
    in_specs = (P("d", None), P("d", None), P("d"), P())
    return jax.shard_map(local, mesh=flat, in_specs=in_specs, out_specs=P("d", None), check_vma=False)
```

time: 788 us -> 91.9 us (0.12)
  the two profiles are of different devices: /device:TPU:1 before, /device:TPU:2 now
where the time goes in v1:
time: 91.9 us; the launch traced here: 91.6 us
  blocking collectives  78.1 us (85%)
  waiting for transfers between devices  4.13 us (4%)
  Pallas kernels  3.87 us (4%)
  local copies, waits for them, and re-layouts  2.17 us (2%)
  starting transfers between devices  1.92 us (2%)
  other arithmetic  1.31 us (1%)
    all_to_all x3, blocking collectives, local(): lax.all_to_all(held, 'd', split_axis=0, concat_axis=0, axis_index_groups=...  78.1 us
    ppermute x1, waiting for transfers between devices, local(): other = lax.ppermute(send, 'd', [(i, i ^ 1) for i in range(ALL)])  4.13 us
    pallas_call x1, Pallas kernels, local(): pl.pallas_call(products, out_shape=[jax.ShapeDtypeStruct((8, 8, 8) + tile...  3.87 us
    unnamed x6, local copies, waits for them, and re-layouts  2.17 us
    ppermute x1, starting transfers between devices, local(): other = lax.ppermute(send, 'd', [(i, i ^ 1) for i in range(ALL)])  1.92 us
  transfers between devices with their start and end apart: 1, of which 1 were waited for; matrix products, arithmetic and copies ran while one was open for 0% of the time, Pallas kernels for 0%

profile of v1, /device:TPU:2, one launch (start us, length us, event | category | flops | bytes accessed | tf_op | source)
XLA Modules:
  0.0 91.6 jit_solution(15205570111152053957)
XLA Ops:
  0.0 0.0 copy-start
  0.0 0.8 copy-done
  0.8 0.0 copy-start.1
  0.8 0.7 copy-done.1
  1.5 0.0 copy-start.2
  1.5 0.7 copy-done.2
  2.2 3.9 %products.1 = (f32[8,8,8,8,128]{4,3,2,1,0:T(8,128)S(1)}, f32[8,8,8,8,128]{4,3,2,1,0:T(8,128)S(1)}) custom-call(s32[2,32]{1,0:T(2,128)S(1)} %copy-done.1, s32[1,128]{1,0:T(1,128)S(1)} %bitcast.1, bf16[128,256]{1,0:T(8,128)(2,1)S(1)} %copy-done, bf16[128,8192]{1,0:T(8,128)(2,1)} %act_ref.1), custom_call_target="tpu_custom_call" | custom-call | tf_op jit(solution)/shard_map/products/pallas_call | solution.py:75
  6.0 1.9 %collective-permute-start = (f32[8,8,8,8,128]{4,3,2,1,0:T(8,128)S(1)}, f32[8,8,8,8,128]{4,3,2,1,0:T(8,128)S(1)}, u32[]{:S(2)}, u32[]{:S(2)}) collective-permute-start(f32[8,8,8,8,128]{4,3,2,1,0:T(8,128)S(1)} %get-tuple-element.8), channel_id=1, source_target_pairs={{0,1},{1,0},{2,3},{3,2},{4,5},{5,4},{6,7},{7,6},{8,9},{9,8},{10,11... | collective-permute-start | bytes 6291464 | tf_op jit(solution)/shard_map/ppermute | solution.py:83
  8.0 4.1 %collective-permute-done = f32[8,8,8,8,128]{4,3,2,1,0:T(8,128)S(1)} collective-permute-done((f32[8,8,8,8,128]{4,3,2,1,0:T(8,128)S(1)}, f32[8,8,8,8,128]{4,3,2,1,0:T(8,128)S(1)}, u32[]{:S(2)}, u32[]{:S(2)}) %collective-permute-start) | collective-permute-done | bytes 2097184 | tf_op jit(solution)/shard_map/ppermute | solution.py:83
  12.1 0.6 add.3
  12.7 44.3 %all_to_all.15 = f32[8,8,8,8,128]{4,3,2,1,0:T(8,128)S(1)} all-to-all(f32[8,8,8,8,128]{4,3,2,1,0:T(8,128)S(1)} %add.3), channel_id=1, replica_groups={{0,64,128,192,256,320,384,448},{1,3,5,7,9,11,13,15},{2,66,130,194,258,3..., dimensions={0} | all-to-all | bytes 4194304 | tf_op jit(solution)/shard_map/all_to_all | solution.py:86
  57.0 0.1 reduce_sum.27
  57.1 12.9 %all_to_all.16 = f32[8,8,8,128]{3,2,1,0:T(8,128)S(1)} all-to-all(f32[8,8,8,128]{3,2,1,0:T(8,128)S(1)} %reduce_sum.27), channel_id=1, replica_groups={{0,2,4,6,8,10,12,14},{1,17,33,49,513,529,545,561},{3,19,35,51,515,531,5..., dimensions={0} | all-to-all | bytes 524288 | tf_op jit(solution)/shard_map/all_to_all | solution.py:86
  70.0 20.9 %all_to_all.17 = f32[8,8,128]{2,1,0:T(8,128)S(1)} all-to-all(f32[8,8,128]{2,1,0:T(8,128)S(1)} %reduce_sum.28), channel_id=1, replica_groups={{0,16,32,48,512,528,544,560},{1,65,129,193,257,321,385,449},{2,18,34,50..., dimensions={0} | all-to-all | bytes 65536 | tf_op jit(solution)/shard_map/all_to_all | solution.py:86
  91.0 0.6 broadcast_multiply_fusion
  (2 shorter events, 0.0 us)
Async XLA Ops:
  0.0 0.8 copy-start
  0.8 0.7 copy-start.1
  1.5 0.7 copy-start.2
  6.0 6.1 %collective-permute-start = (f32[8,8,8,8,128]{4,3,2,1,0:T(8,128)S(1)}, f32[8,8,8,8,128]{4,3,2,1,0:T(8,128)S(1)}, u32[]{:S(2)}, u32[]{:S(2)}) collective-permute-start(f32[8,8,8,8,128]{4,3,2,1,0:T(8,128)S(1)} %get-tuple-element.8), channel_id=1, source_target_pairs={{0,1},{1,0},{2,3},{3,2},{4,5},{5,4},{6,7},{7,6},{8,9},{9,8},{10,11... | collective-permute-start | bytes 6291464 | tf_op jit(solution)/shard_map/ppermute | solution.py:83

commit v2 on v1

--- a/solution.py
+++ b/solution.py
@@ -18,23 +18,26 @@
     return (((z // ZL * X + x) * ZL + z % ZL) * Y + y) * C + c
 
 
-def line(axis, x, y, z, c):
-    if axis == "x":
-        return [number(i, y, z, c) for i in range(X)]
-    if axis == "y":
-        return [number(x, i, z, c) for i in range(Y)]
-    return [number(x, y, i, c) for i in range(Z)]
+def cubes():
+    groups = []
+    for c in range(C):
+        for x in range(c, X, 2):
+            for y in range(c, Y, 2):
+                for z in range(c, Z, 2):
+                    members = [((x + i) % X, (y + j) % Y, (z + k) % Z) for i in range(2) for j in range(2) for k in range(2)]
+                    members.sort(key=lambda m: (m[0] % 2, m[1] % 2, m[2] % 2))
+                    groups.append([number(*m, c) for m in members])
+    return groups
 
 
-def lines(axis_of_core):
-    groups = {
-        tuple(line(axis_of_core[c], x, y, z, c))
-        for x in range(X)
-        for y in range(Y)
-        for z in range(Z)
+def lattices():
+    return [
+        [number(x, y, z, c) for x in range(i, X, 2) for y in range(j, Y, 2) for z in range(k, Z, 2)]
         for c in range(C)
-    }
-    return [list(g) for g in sorted(groups)]
+        for i in range(2)
+        for j in range(2)
+        for k in range(2)
+    ]
 
 
 def products(kept_ref, ids_ref, grad_ref, act_ref, mine_ref, send_ref):
@@ -57,9 +60,10 @@
                 block = act_ref[:, pl.ds(start, width)]
                 sums = lax.dot_general(
                     block, targets[j], (((0,), (0,)), ((), ())), preferred_element_type=jnp.float32
-                ).reshape(Y, C, ROWS, width)
-                zero_ref[x, :, z] = sums[:, 0]
-                one_ref[:, z, x] = sums[:, 1]
+                ).reshape(Y // 2, 2, C, ROWS, width)
+                for odd in range(2):
+                    zero_ref[x % 2, odd, z % 2, x // 2, :, z // 2] = sums[:, odd, 0]
+                    one_ref[x % 2, odd, z % 2, x // 2, :, z // 2] = sums[:, odd, 1]
             return carry
 
         lax.fori_loop(0, X * ZL, step, 0, unroll=4)
@@ -74,19 +78,18 @@
     vmem = pl.BlockSpec(memory_space=pltpu.VMEM)
     mine, send = pl.pallas_call(
         products,
-        out_shape=[jax.ShapeDtypeStruct((8, 8, 8) + tile, jnp.float32)] * 2,
+        out_shape=[jax.ShapeDtypeStruct((2, 2, 2, X // 2, Y // 2, Z // 2) + tile, jnp.float32)] * 2,
         in_specs=[pl.BlockSpec(memory_space=pltpu.SMEM), vmem, vmem, vmem],
         out_specs=[vmem, vmem],
         compiler_params=pltpu.CompilerParams(vmem_limit_bytes=48 * 1024 * 1024),
         name="products",
     )(kept_rows, token_ids.reshape(1, tokens), cotangent, activations)
     other = lax.ppermute(send, "d", [(i, i ^ 1) for i in range(ALL)])
-    held = mine + other
-    for axes in (("x", "y"), ("y", "z"), ("z", "x")):
-        parts = lax.all_to_all(
-            held, "d", split_axis=0, concat_axis=0, axis_index_groups=lines(axes), tiled=True
-        )
-        held = jnp.sum(parts, axis=0)
+    held = (mine + other).reshape((-1,) + tile)
+    for groups in (cubes(), lattices()):
+        parts = lax.all_to_all(held, "d", split_axis=0, concat_axis=0, axis_index_groups=groups, tiled=True)
+        held = jnp.sum(parts.reshape((len(groups[0]), -1) + tile), axis=0)
+    held = held.reshape(tile)
     return held * jnp.float32(1.0 / math.sqrt(tokens * ALL))
 
 

time: 91.9 us -> 82.4 us (0.90)
  the two profiles are of different devices: /device:TPU:2 before, /device:TPU:1 now
where the time goes in v2:
time: 82.4 us; the launch traced here: 82.1 us
  blocking collectives  54.6 us (66%)
  starting transfers between devices  16 us (19%)
  Pallas kernels  4.1 us (5%)
  waiting for transfers between devices  3.76 us (5%)
  local copies, waits for them, and re-layouts  2.17 us (3%)
  other arithmetic  1.4 us (2%)
    all_to_all x2, blocking collectives, local(): lax.all_to_all(held, 'd', split_axis=0, concat_axis=0, axis_index_groups=...  54.6 us
    ppermute x1, starting transfers between devices, local(): other = lax.ppermute(send, 'd', [(i, i ^ 1) for i in range(ALL)])  16 us
    pallas_call x1, Pallas kernels, local(): pl.pallas_call(products, out_shape=[jax.ShapeDtypeStruct((2, 2, 2, X // 2...  4.1 us
    ppermute x1, waiting for transfers between devices, local(): other = lax.ppermute(send, 'd', [(i, i ^ 1) for i in range(ALL)])  3.76 us
    unnamed x6, local copies, waits for them, and re-layouts  2.17 us
  transfers between devices with their start and end apart: 1, of which 1 were waited for; matrix products, arithmetic and copies ran while one was open for 0% of the time, Pallas kernels for 0%

profile of v2, /device:TPU:1, one launch (start us, length us, event | category | flops | bytes accessed | tf_op | source)
XLA Modules:
  0.0 82.1 jit_solution(7638889363572315256)
XLA Ops:
  0.0 0.0 copy-start
  0.0 0.8 %copy-done = bf16[128,256]{1,0:T(8,128)(2,1)S(1)} copy-done((bf16[128,256]{1,0:T(8,128)(2,1)S(1)}, bf16[128,256]{1,0:T(8,128)(2,1)}, u32[]{:S(2)}) %copy-start) | copy-done | bytes 65560
  0.8 0.0 copy-start.1
  0.8 0.7 copy-done.1
  1.5 0.0 copy-start.2
  1.5 0.7 copy-done.2
  2.2 4.1 %products.1 = (f32[2,2,2,4,4,4,8,128]{7,6,5,4,3,2,1,0:T(8,128)S(1)}, f32[2,2,2,4,4,4,8,128]{7,6,5,4,3,2,1,0:T(8,128)S(1)}) custom-call(s32[2,32]{1,0:T(2,128)S(1)} %copy-done.1, s32[1,128]{1,0:T(1,128)S(1)} %bitcast.3, bf16[128,256]{1,0:T(8,128)(2,1)S(1)} %copy-done, bf16[128,8192]{1,0:T(8,128)(2,1)} %act_ref.1), custom_call_target="tpu_custom_call" | custom-call | tf_op jit(solution)/shard_map/products/pallas_call | solution.py:79
  6.3 16.0 %collective-permute-start = (f32[2,2,2,4,4,4,8,128]{7,6,5,4,3,2,1,0:T(8,128)S(1)}, f32[2,2,2,4,4,4,8,128]{7,6,5,4,3,2,1,0:T(8,128)S(1)}, u32[]{:S(2)}, u32[]{:S(2)}) collective-permute-start(f32[2,2,2,4,4,4,8,128]{7,6,5,4,3,2,1,0:T(8,128)S(1)} %get-tuple-element.8), channel_id=1, source_target_pairs={{0,1},{1,0},{2,3},{3,2},{4,5},{5,4},{6,7},{7,6},{8,9},{9,8},{10,11... | collective-permute-start | bytes 6291464 | tf_op jit(solution)/shard_map/ppermute | solution.py:87
  22.3 3.8 %collective-permute-done = f32[2,2,2,4,4,4,8,128]{7,6,5,4,3,2,1,0:T(8,128)S(1)} collective-permute-done((f32[2,2,2,4,4,4,8,128]{7,6,5,4,3,2,1,0:T(8,128)S(1)}, f32[2,2,2,4,4,4,8,128]{7,6,5,4,3,2,1,0:T(8,128)S(1)}, u32[]{:S(2)}, u32[]{:S(2)}) %collective-permute-start) | collective-permute-done | bytes 2097184 | tf_op jit(solution)/shard_map/ppermute | solution.py:87
  26.1 0.6 add.3
  26.7 28.5 %all_to_all.10 = f32[512,8,128]{2,1,0:T(8,128)S(1)} all-to-all(f32[512,8,128]{2,1,0:T(8,128)S(1)} %bitcast.4), channel_id=1, replica_groups={{0,16,2,18,64,80,66,82},{32,48,34,50,96,112,98,114},{512,528,514,530,57..., dimensions={0} | all-to-all | bytes 4194304 | tf_op jit(solution)/shard_map/all_to_all | solution.py:90
  55.2 0.1 reduce_sum.18
  55.3 26.1 %all_to_all.11 = f32[64,8,128]{2,1,0:T(8,128)S(1)} all-to-all(f32[64,8,128]{2,1,0:T(8,128)S(1)} %reduce_sum.18), channel_id=1, replica_groups={{0,32,512,544,4,36,516,548,8,40,520,552,12,44,524,556,128,160,640,672,1..., dimensions={0} | all-to-all | bytes 524288 | tf_op jit(solution)/shard_map/all_to_all | solution.py:90
  81.4 0.1 reduce_sum.19
  81.5 0.6 broadcast_multiply_fusion
Async XLA Ops:
  0.0 0.8 %copy-start = (bf16[128,256]{1,0:T(8,128)(2,1)S(1)}, bf16[128,256]{1,0:T(8,128)(2,1)}, u32[]{:S(2)}) copy-start(bf16[128,256]{1,0:T(8,128)(2,1)} %grad_ref.1) | copy-start | bytes 196612
  0.8 0.7 copy-start.1
  1.5 0.7 copy-start.2
  6.3 19.8 %collective-permute-start = (f32[2,2,2,4,4,4,8,128]{7,6,5,4,3,2,1,0:T(8,128)S(1)}, f32[2,2,2,4,4,4,8,128]{7,6,5,4,3,2,1,0:T(8,128)S(1)}, u32[]{:S(2)}, u32[]{:S(2)}) collective-permute-start(f32[2,2,2,4,4,4,8,128]{7,6,5,4,3,2,1,0:T(8,128)S(1)} %get-tuple-element.8), channel_id=1, source_target_pairs={{0,1},{1,0},{2,3},{3,2},{4,5},{5,4},{6,7},{7,6},{8,9},{9,8},{10,11... | collective-permute-start | bytes 6291464 | tf_op jit(solution)/shard_map/ppermute | solution.py:87

commit v3 on v2

v3 whole, which is shorter than its diff:
```python
import math

import jax
import jax.numpy as jnp
import numpy as np
from jax import lax
from jax.experimental import pallas as pl
from jax.experimental.pallas import tpu as pltpu
from jax.sharding import Mesh, PartitionSpec as P

ZH, X, ZL, Y, C = 2, 8, 4, 8, 2
Z = ZH * ZL
ALL = ZH * X * ZL * Y * C
ROWS = 8


def number(x, y, z, c):
    return (((z // ZL * X + x) * ZL + z % ZL) * Y + y) * C + c


def bit(value, at):
    return value >> at & 1


def exchanges():
    keys = []
    for c in range(C):
        first = lambda x, y, z, c=c: (c, (x - c) % X // 2, (y - c) % Y // 2, (z - c) % Z // 2)
        keys.append(first)
    found = [{}, {}, {}]
    for c in range(C):
        for x in range(X):
            for y in range(Y):
                for z in range(Z):
                    a, b, d = (x, y, z) if c == 0 else (y, z, x)
                    odd = (x % 2, y % 2, z % 2)
                    second, third = (a // 2, bit(b, 1)), (d // 2, bit(b, 2))
                    for groups, group, place in zip(
                        found,
                        (keys[c](x, y, z), (c, odd, third), (c, odd, second)),
                        (odd, second, third),
                        strict=True,
                    ):
                        groups.setdefault(group, []).append((place, number(x, y, z, c)))
    return [[[n for _, n in sorted(g)] for g in groups.values()] for groups in found]


def products(kept_any, ids_any, grad_any, act_any, mine_ref, send_ref, kept_ref, ids_ref, grad_ref, act_ref, sems):
    copies = [
        pltpu.make_async_copy(src, dst, sems.at[i])
        for i, (src, dst) in enumerate(
            ((act_any, act_ref), (kept_any, kept_ref), (ids_any, ids_ref), (grad_any, grad_ref))
        )
    ]
    for copy in copies:
        copy.start()
    core = lax.rem(lax.axis_index("d"), C)
    tokens, width = act_ref.shape[0], grad_ref.shape[1] // ZH
    scale = 1.0 / math.sqrt(tokens * ALL)
    for copy in copies[1:]:
        copy.wait()
    live = jnp.transpose(jnp.broadcast_to(ids_ref[...], (width, tokens))) != 0
    targets = [
        jnp.where(live, grad_ref[:, j * width:(j + 1) * width].astype(jnp.float32), 0.0).astype(jnp.bfloat16)
        for j in range(ZH)
    ]
    copies[0].wait()

    def run(own):
        zero_ref, one_ref = (mine_ref, send_ref) if own == 0 else (send_ref, mine_ref)

        def step(k, carry):
            x, zl = k // ZL, lax.rem(k, ZL)
            xo, xh, zo, z1 = x % 2, x // 2, zl % 2, zl // 2
            for j in range(ZH):
                start = pl.multiple_of(kept_ref[j, k] * width, width)
                block = act_ref[:, pl.ds(start, width)]
                sums = lax.dot_general(
                    block, targets[j], (((0,), (0,)), ((), ())), preferred_element_type=jnp.float32
                ) * jnp.float32(scale)
                sums = sums.reshape(Y // 2, 2, C, ROWS, width)
                for yo in range(2):
                    one_ref[xo, yo, zo, :, z1, xh, j] = sums[:, yo, 1]
                    halves = sums[:, yo, 0].reshape(2, 2, ROWS, width)
                    for y1 in range(2):
                        zero_ref[xo, yo, zo, xh, y1, j * 2 + z1] = halves[:, y1]
            return carry

        lax.fori_loop(0, X * ZL, step, 0, unroll=4)

    pl.when(core == 0)(lambda: run(0))
    pl.when(core == 1)(lambda: run(1))


def local(activations, cotangent, token_ids, kept_rows):
    tokens = activations.shape[0]
    tile = (ROWS, cotangent.shape[1] // ZH)
    vmem, hbm = pl.BlockSpec(memory_space=pltpu.VMEM), pl.BlockSpec(memory_space=pltpu.HBM)
    mine, send = pl.pallas_call(
        products,
        out_shape=[jax.ShapeDtypeStruct((2, 2, 2, 4, 2, 4, 2) + tile, jnp.float32)] * 2,
        in_specs=[hbm] * 4,
        out_specs=[vmem, vmem],
        scratch_shapes=[
            pltpu.SMEM(kept_rows.shape, jnp.int32),
            pltpu.VMEM((1, tokens), jnp.int32),
            pltpu.VMEM(cotangent.shape, jnp.bfloat16),
            pltpu.VMEM(activations.shape, jnp.bfloat16),
            pltpu.SemaphoreType.DMA((4,)),
        ],
        compiler_params=pltpu.CompilerParams(vmem_limit_bytes=48 * 1024 * 1024),
        name="products",
    )(*(
        pltpu.with_memory_space_constraint(a, pltpu.HBM)
        for a in (kept_rows, token_ids.reshape(1, tokens), cotangent, activations)
    ))
    other = lax.ppermute(send, "d", [(i, i ^ 1) for i in range(ALL)])
    held = (mine + other).reshape((-1,) + tile)
    for groups in exchanges():
        parts = lax.all_to_all(held, "d", split_axis=0, concat_axis=0, axis_index_groups=groups, tiled=True)
        held = jnp.sum(parts.reshape((len(groups[0]), -1) + tile), axis=0)
    return held.reshape(tile)


def solution(mesh):
    flat = Mesh(np.asarray(mesh.devices).reshape(-1), ("d",))
    in_specs = (P("d", None), P("d", None), P("d"), P())
    return jax.shard_map(local, mesh=flat, in_specs=in_specs, out_specs=P("d", None), check_vma=False)
```

time: 82.4 us -> 83.9 us (1.018)
  blocking collectives: 54.6 us -> 58.7 us
  local copies, waits for them, and re-layouts: 2.17 us -> 0 us
    all_to_all x2 -> x3, blocking collectives: 54.6 us -> 58.7 us  [local(): lax.all_to_all(held, 'd', split_axis=0, concat_axis=0, axis_index_groups=...]
    unnamed x6 -> x0, local copies, waits for them, and re-layouts: 2.17 us -> none
where the time goes in v3:
time: 83.9 us; the launch traced here: 83.7 us
  blocking collectives  58.7 us (70%)
  starting transfers between devices  16.1 us (19%)
  Pallas kernels  3.92 us (5%)
  waiting for transfers between devices  3.76 us (4%)
  other arithmetic  1.17 us (1%)
    all_to_all x3, blocking collectives, local(): lax.all_to_all(held, 'd', split_axis=0, concat_axis=0, axis_index_groups=...  58.7 us
    ppermute x1, starting transfers between devices, local(): other = lax.ppermute(send, 'd', [(i, i ^ 1) for i in range(ALL)])  16.1 us
    pallas_call x1, Pallas kernels, local(): pl.pallas_call(products, out_shape=[jax.ShapeDtypeStruct((2, 2, 2, 4, 2,...  3.92 us
    ppermute x1, waiting for transfers between devices, local(): other = lax.ppermute(send, 'd', [(i, i ^ 1) for i in range(ALL)])  3.76 us
  transfers between devices with their start and end apart: 1, of which 1 were waited for; matrix products, arithmetic and copies ran while one was open for 0% of the time, Pallas kernels for 0%

profile of v3, /device:TPU:1, one launch (start us, length us, event | category | flops | bytes accessed | tf_op | source)
XLA Modules:
  0.0 83.7 jit_solution(18045091184295098088)
XLA Ops:
  0.0 3.9 %products.1 = (f32[2,2,2,4,2,4,2,8,128]{8,7,6,5,4,3,2,1,0:T(8,128)S(1)}, f32[2,2,2,4,2,4,2,8,128]{8,7,6,5,4,3,2,1,0:T(8,128)S(1)}) custom-call(s32[2,32]{1,0:T(2,128)} %kept_any.1, s32[1,128]{1,0:T(1,128)} %bitcast.7, bf16[128,256]{1,0:T(8,128)(2,1)} %grad_any.1, bf16[128,8192]{1,0:T(8,128)(2,1)} %act_any.1), custom_call_target="tpu_custom_call" | custom-call | tf_op jit(solution)/shard_map/products/pallas_call | solution.py:99
  3.9 16.1 %collective-permute-start = (f32[2,2,2,4,2,4,2,8,128]{8,7,6,5,4,3,2,1,0:T(8,128)S(1)}, f32[2,2,2,4,2,4,2,8,128]{8,7,6,5,4,3,2,1,0:T(8,128)S(1)}, u32[]{:S(2)}, u32[]{:S(2)}) collective-permute-start(f32[2,2,2,4,2,4,2,8,128]{8,7,6,5,4,3,2,1,0:T(8,128)S(1)} %get-tuple-element.8), channel_id=1, source_target_pairs={{0,1},{1,0},{2,3},{3,2},{4,5},{5,4},{6,7},{7,6},{8,9},{9,8},{10,11... | collective-permute-start | bytes 6291464 | tf_op jit(solution)/shard_map/ppermute | solution.py:117
  20.0 3.8 %collective-permute-done = f32[2,2,2,4,2,4,2,8,128]{8,7,6,5,4,3,2,1,0:T(8,128)S(1)} collective-permute-done((f32[2,2,2,4,2,4,2,8,128]{8,7,6,5,4,3,2,1,0:T(8,128)S(1)}, f32[2,2,2,4,2,4,2,8,128]{8,7,6,5,4,3,2,1,0:T(8,128)S(1)}, u32[]{:S(2)}, u32[]{:S(2)}) %collective-permute-start) | collective-permute-done | bytes 2097184 | tf_op jit(solution)/shard_map/ppermute | solution.py:117
  23.8 0.4 add.3
  24.2 28.5 %all_to_all.15 = f32[512,8,128]{2,1,0:T(8,128)S(1)} all-to-all(f32[512,8,128]{2,1,0:T(8,128)S(1)} %bitcast.4), channel_id=1, replica_groups={{0,16,2,18,64,80,66,82},{32,48,34,50,96,112,98,114},{512,528,514,530,57..., dimensions={0} | all-to-all | bytes 4194304 | tf_op jit(solution)/shard_map/all_to_all | solution.py:120
  52.7 0.1 reduce_sum.27
  52.8 12.4 %all_to_all.16 = f32[64,8,128]{2,1,0:T(8,128)S(1)} all-to-all(f32[64,8,128]{2,1,0:T(8,128)S(1)} %reduce_sum.27), channel_id=1, replica_groups={{0,4,128,132,256,260,384,388},{16,20,144,148,272,276,400,404},{32,36,16..., dimensions={0} | all-to-all | bytes 524288 | tf_op jit(solution)/shard_map/all_to_all | solution.py:120
  65.2 17.8 %all_to_all.17 = f32[8,8,128]{2,1,0:T(8,128)S(1)} all-to-all(f32[8,8,128]{2,1,0:T(8,128)S(1)} %reduce_sum.28), channel_id=1, replica_groups={{0,8,32,40,512,520,544,552},{16,24,48,56,528,536,560,568},{2,10,34,42,5..., dimensions={0} | all-to-all | bytes 65536 | tf_op jit(solution)/shard_map/all_to_all | solution.py:120
  83.1 0.6 reduce_sum.29
  (1 shorter events, 0.0 us)
Async XLA Ops:
  3.9 19.8 %collective-permute-start = (f32[2,2,2,4,2,4,2,8,128]{8,7,6,5,4,3,2,1,0:T(8,128)S(1)}, f32[2,2,2,4,2,4,2,8,128]{8,7,6,5,4,3,2,1,0:T(8,128)S(1)}, u32[]{:S(2)}, u32[]{:S(2)}) collective-permute-start(f32[2,2,2,4,2,4,2,8,128]{8,7,6,5,4,3,2,1,0:T(8,128)S(1)} %get-tuple-element.8), channel_id=1, source_target_pairs={{0,1},{1,0},{2,3},{3,2},{4,5},{5,4},{6,7},{7,6},{8,9},{9,8},{10,11... | collective-permute-start | bytes 6291464 | tf_op jit(solution)/shard_map/ppermute | solution.py:117

commit v4 on v3

--- a/solution.py
+++ b/solution.py
@@ -18,31 +18,25 @@
     return (((z // ZL * X + x) * ZL + z % ZL) * Y + y) * C + c
 
 
-def bit(value, at):
-    return value >> at & 1
+def half(place):
+    return (place ^ place >> 1 ^ place >> 2) & 1
+
+
+def order(x, y, z):
+    return half(x) * 4 + half(y) * 2 + half(z), x // 2 * 16 + y // 2 * 4 + z // 2
 
 
 def exchanges():
-    keys = []
-    for c in range(C):
-        first = lambda x, y, z, c=c: (c, (x - c) % X // 2, (y - c) % Y // 2, (z - c) % Z // 2)
-        keys.append(first)
-    found = [{}, {}, {}]
+    cubes, lattices = {}, {}
     for c in range(C):
         for x in range(X):
             for y in range(Y):
                 for z in range(Z):
-                    a, b, d = (x, y, z) if c == 0 else (y, z, x)
-                    odd = (x % 2, y % 2, z % 2)
-                    second, third = (a // 2, bit(b, 1)), (d // 2, bit(b, 2))
-                    for groups, group, place in zip(
-                        found,
-                        (keys[c](x, y, z), (c, odd, third), (c, odd, second)),
-                        (odd, second, third),
-                        strict=True,
-                    ):
-                        groups.setdefault(group, []).append((place, number(x, y, z, c)))
-    return [[[n for _, n in sorted(g)] for g in groups.values()] for groups in found]
+                    first, second = order(x, y, z)
+                    device = number((x + c) % X, (y + c) % Y, (z + c) % Z, c)
+                    cubes.setdefault((c, second), []).append((first, device))
+                    lattices.setdefault((c, first), []).append((second, device))
+    return [[[n for _, n in sorted(g)] for g in groups.values()] for groups in (cubes, lattices)]
 
 
 def products(kept_any, ids_any, grad_any, act_any, mine_ref, send_ref, kept_ref, ids_ref, grad_ref, act_ref, sems):
@@ -69,24 +63,22 @@
     def run(own):
         zero_ref, one_ref = (mine_ref, send_ref) if own == 0 else (send_ref, mine_ref)
 
-        def step(k, carry):
-            x, zl = k // ZL, lax.rem(k, ZL)
-            xo, xh, zo, z1 = x % 2, x // 2, zl % 2, zl // 2
-            for j in range(ZH):
+        def step(x, carry):
+            for z in range(Z):
+                j, k = z // ZL, x * ZL + z % ZL
                 start = pl.multiple_of(kept_ref[j, k] * width, width)
                 block = act_ref[:, pl.ds(start, width)]
                 sums = lax.dot_general(
                     block, targets[j], (((0,), (0,)), ((), ())), preferred_element_type=jnp.float32
                 ) * jnp.float32(scale)
-                sums = sums.reshape(Y // 2, 2, C, ROWS, width)
-                for yo in range(2):
-                    one_ref[xo, yo, zo, :, z1, xh, j] = sums[:, yo, 1]
-                    halves = sums[:, yo, 0].reshape(2, 2, ROWS, width)
-                    for y1 in range(2):
-                        zero_ref[xo, yo, zo, xh, y1, j * 2 + z1] = halves[:, y1]
+                sums = sums.reshape(Y, C, ROWS, width)
+                for c, ref in enumerate((zero_ref, one_ref)):
+                    xc, zc = (x + X - c) % X, (z - c) % Z
+                    for y in range(Y):
+                        ref[order(xc, (y - c) % Y, zc)] = sums[y, c]
             return carry
 
-        lax.fori_loop(0, X * ZL, step, 0, unroll=4)
+        lax.fori_loop(0, X, step, 0)
 
     pl.when(core == 0)(lambda: run(0))
     pl.when(core == 1)(lambda: run(1))
@@ -98,7 +90,7 @@
     vmem, hbm = pl.BlockSpec(memory_space=pltpu.VMEM), pl.BlockSpec(memory_space=pltpu.HBM)
     mine, send = pl.pallas_call(
         products,
-        out_shape=[jax.ShapeDtypeStruct((2, 2, 2, 4, 2, 4, 2) + tile, jnp.float32)] * 2,
+        out_shape=[jax.ShapeDtypeStruct((8, ALL // C // 8) + tile, jnp.float32)] * 2,
         in_specs=[hbm] * 4,
         out_specs=[vmem, vmem],
         scratch_shapes=[

time: 83.9 us -> 74.2 us (0.88)
  the two profiles are of different devices: /device:TPU:1 before, /device:TPU:2 now
where the time goes in v4:
time: 74.2 us; the launch traced here: 73.9 us
  blocking collectives  63 us (85%)
  waiting for transfers between devices  4.13 us (6%)
  Pallas kernels  3.85 us (5%)
  starting transfers between devices  1.92 us (3%)
  other arithmetic  1.04 us (1%)
    all_to_all x2, blocking collectives, local(): lax.all_to_all(held, 'd', split_axis=0, concat_axis=0, axis_index_groups=...  63 us
    ppermute x1, waiting for transfers between devices, local(): other = lax.ppermute(send, 'd', [(i, i ^ 1) for i in range(ALL)])  4.13 us
    pallas_call x1, Pallas kernels, local(): pl.pallas_call(products, out_shape=[jax.ShapeDtypeStruct((8, ALL // C //...  3.85 us
    ppermute x1, starting transfers between devices, local(): other = lax.ppermute(send, 'd', [(i, i ^ 1) for i in range(ALL)])  1.92 us
  transfers between devices with their start and end apart: 1, of which 1 were waited for; matrix products, arithmetic and copies ran while one was open for 0% of the time, Pallas kernels for 0%

profile of v4, /device:TPU:2, one launch (start us, length us, event | category | flops | bytes accessed | tf_op | source)
XLA Modules:
  0.0 73.9 jit_solution(12041727315988357499)
XLA Ops:
  0.0 3.9 %products.1 = (f32[8,64,8,128]{3,2,1,0:T(8,128)S(1)}, f32[8,64,8,128]{3,2,1,0:T(8,128)S(1)}) custom-call(s32[2,32]{1,0:T(2,128)} %kept_any.1, s32[1,128]{1,0:T(1,128)} %bitcast.5, bf16[128,256]{1,0:T(8,128)(2,1)} %grad_any.1, bf16[128,8192]{1,0:T(8,128)(2,1)} %act_any.1), custom_call_target="tpu_custom_call" | custom-call | tf_op jit(solution)/shard_map/products/pallas_call | solution.py:91
  3.9 1.9 %collective-permute-start = (f32[8,64,8,128]{3,2,1,0:T(8,128)S(1)}, f32[8,64,8,128]{3,2,1,0:T(8,128)S(1)}, u32[]{:S(2)}, u32[]{:S(2)}) collective-permute-start(f32[8,64,8,128]{3,2,1,0:T(8,128)S(1)} %get-tuple-element.8), channel_id=1, source_target_pairs={{0,1},{1,0},{2,3},{3,2},{4,5},{5,4},{6,7},{7,6},{8,9},{9,8},{10,11... | collective-permute-start | bytes 6291464 | tf_op jit(solution)/shard_map/ppermute | solution.py:109
  5.8 4.1 %collective-permute-done = f32[8,64,8,128]{3,2,1,0:T(8,128)S(1)} collective-permute-done((f32[8,64,8,128]{3,2,1,0:T(8,128)S(1)}, f32[8,64,8,128]{3,2,1,0:T(8,128)S(1)}, u32[]{:S(2)}, u32[]{:S(2)}) %collective-permute-start) | collective-permute-done | bytes 2097184 | tf_op jit(solution)/shard_map/ppermute | solution.py:109
  9.9 0.3 add.3
  10.2 31.0 %all_to_all.10 = f32[512,8,128]{2,1,0:T(8,128)S(1)} all-to-all(f32[512,8,128]{2,1,0:T(8,128)S(1)} %bitcast.3), channel_id=1, replica_groups={{0,16,2,18,64,80,66,82},{48,32,50,34,112,96,114,98},{528,512,530,514,59..., dimensions={0} | all-to-all | bytes 4194304 | tf_op jit(solution)/shard_map/all_to_all | solution.py:112
  41.2 0.1 reduce_sum.18
  41.3 32.0 %all_to_all.11 = f32[64,8,128]{2,1,0:T(8,128)S(1)} all-to-all(f32[64,8,128]{2,1,0:T(8,128)S(1)} %reduce_sum.18), channel_id=1, replica_groups={{0,48,528,544,6,54,534,550,10,58,538,554,12,60,540,556,192,240,720,736,..., dimensions={0} | all-to-all | bytes 524288 | tf_op jit(solution)/shard_map/all_to_all | solution.py:112
  73.3 0.7 reduce_sum.19
Async XLA Ops:
  3.9 6.1 %collective-permute-start = (f32[8,64,8,128]{3,2,1,0:T(8,128)S(1)}, f32[8,64,8,128]{3,2,1,0:T(8,128)S(1)}, u32[]{:S(2)}, u32[]{:S(2)}) collective-permute-start(f32[8,64,8,128]{3,2,1,0:T(8,128)S(1)} %get-tuple-element.8), channel_id=1, source_target_pairs={{0,1},{1,0},{2,3},{3,2},{4,5},{5,4},{6,7},{7,6},{8,9},{9,8},{10,11... | collective-permute-start | bytes 6291464 | tf_op jit(solution)/shard_map/ppermute | solution.py:109

commit v5 on v4

--- a/solution.py
+++ b/solution.py
@@ -78,7 +78,7 @@
                         ref[order(xc, (y - c) % Y, zc)] = sums[y, c]
             return carry
 
-        lax.fori_loop(0, X, step, 0)
+        lax.fori_loop(0, X, step, 0, unroll=True)
 
     pl.when(core == 0)(lambda: run(0))
     pl.when(core == 1)(lambda: run(1))

time: 74.2 us -> 72.7 us (0.980)
  Pallas kernels: 3.85 us -> 2.39 us
    pallas_call x1, Pallas kernels: 3.85 us -> 2.39 us  [local(): pl.pallas_call(products, out_shape=[jax.ShapeDtypeStruct((8, ALL // C //...]
where the time goes in v5:
time: 72.7 us; the launch traced here: 72.5 us
  blocking collectives  63 us (87%)
  waiting for transfers between devices  4.13 us (6%)
  Pallas kernels  2.39 us (3%)
  starting transfers between devices  1.92 us (3%)
  other arithmetic  1.04 us (1%)
    all_to_all x2, blocking collectives, local(): lax.all_to_all(held, 'd', split_axis=0, concat_axis=0, axis_index_groups=...  63 us
    ppermute x1, waiting for transfers between devices, local(): other = lax.ppermute(send, 'd', [(i, i ^ 1) for i in range(ALL)])  4.13 us
    pallas_call x1, Pallas kernels, local(): pl.pallas_call(products, out_shape=[jax.ShapeDtypeStruct((8, ALL // C //...  2.39 us
    ppermute x1, starting transfers between devices, local(): other = lax.ppermute(send, 'd', [(i, i ^ 1) for i in range(ALL)])  1.92 us
  transfers between devices with their start and end apart: 1, of which 1 were waited for; matrix products, arithmetic and copies ran while one was open for 0% of the time, Pallas kernels for 0%

profile of v5, /device:TPU:2, one launch (start us, length us, event | category | flops | bytes accessed | tf_op | source)
XLA Modules:
  0.0 72.5 jit_solution(13026338295478836981)
XLA Ops:
  0.0 2.4 %products.1 = (f32[8,64,8,128]{3,2,1,0:T(8,128)S(1)}, f32[8,64,8,128]{3,2,1,0:T(8,128)S(1)}) custom-call(s32[2,32]{1,0:T(2,128)} %kept_any.1, s32[1,128]{1,0:T(1,128)} %bitcast.5, bf16[128,256]{1,0:T(8,128)(2,1)} %grad_any.1, bf16[128,8192]{1,0:T(8,128)(2,1)} %act_any.1), custom_call_target="tpu_custom_call" | custom-call | tf_op jit(solution)/shard_map/products/pallas_call | solution.py:91
  2.4 1.9 %collective-permute-start = (f32[8,64,8,128]{3,2,1,0:T(8,128)S(1)}, f32[8,64,8,128]{3,2,1,0:T(8,128)S(1)}, u32[]{:S(2)}, u32[]{:S(2)}) collective-permute-start(f32[8,64,8,128]{3,2,1,0:T(8,128)S(1)} %get-tuple-element.8), channel_id=1, source_target_pairs={{0,1},{1,0},{2,3},{3,2},{4,5},{5,4},{6,7},{7,6},{8,9},{9,8},{10,11... | collective-permute-start | bytes 6291464 | tf_op jit(solution)/shard_map/ppermute | solution.py:109
  4.3 4.1 %collective-permute-done = f32[8,64,8,128]{3,2,1,0:T(8,128)S(1)} collective-permute-done((f32[8,64,8,128]{3,2,1,0:T(8,128)S(1)}, f32[8,64,8,128]{3,2,1,0:T(8,128)S(1)}, u32[]{:S(2)}, u32[]{:S(2)}) %collective-permute-start) | collective-permute-done | bytes 2097184 | tf_op jit(solution)/shard_map/ppermute | solution.py:109
  8.5 0.3 add.3
  8.7 31.0 %all_to_all.10 = f32[512,8,128]{2,1,0:T(8,128)S(1)} all-to-all(f32[512,8,128]{2,1,0:T(8,128)S(1)} %bitcast.3), channel_id=1, replica_groups={{0,16,2,18,64,80,66,82},{48,32,50,34,112,96,114,98},{528,512,530,514,59..., dimensions={0} | all-to-all | bytes 4194304 | tf_op jit(solution)/shard_map/all_to_all | solution.py:112
  39.7 0.1 reduce_sum.18
  39.8 32.0 %all_to_all.11 = f32[64,8,128]{2,1,0:T(8,128)S(1)} all-to-all(f32[64,8,128]{2,1,0:T(8,128)S(1)} %reduce_sum.18), channel_id=1, replica_groups={{0,48,528,544,6,54,534,550,10,58,538,554,12,60,540,556,192,240,720,736,..., dimensions={0} | all-to-all | bytes 524288 | tf_op jit(solution)/shard_map/all_to_all | solution.py:112
  71.8 0.7 reduce_sum.19
Async XLA Ops:
  2.4 6.1 %collective-permute-start = (f32[8,64,8,128]{3,2,1,0:T(8,128)S(1)}, f32[8,64,8,128]{3,2,1,0:T(8,128)S(1)}, u32[]{:S(2)}, u32[]{:S(2)}) collective-permute-start(f32[8,64,8,128]{3,2,1,0:T(8,128)S(1)} %get-tuple-element.8), channel_id=1, source_target_pairs={{0,1},{1,0},{2,3},{3,2},{4,5},{5,4},{6,7},{7,6},{8,9},{9,8},{10,11... | collective-permute-start | bytes 6291464 | tf_op jit(solution)/shard_map/ppermute | solution.py:109

commit v6 on v5

--- a/solution.py
+++ b/solution.py
@@ -12,6 +12,7 @@
 Z = ZH * ZL
 ALL = ZH * X * ZL * Y * C
 ROWS = 8
+START = ((0, 1, 1), (1, 0, 0))
 
 
 def number(x, y, z, c):
@@ -33,7 +34,7 @@
             for y in range(Y):
                 for z in range(Z):
                     first, second = order(x, y, z)
-                    device = number((x + c) % X, (y + c) % Y, (z + c) % Z, c)
+                    device = number((x + START[c][0]) % X, (y + START[c][1]) % Y, (z + START[c][2]) % Z, c)
                     cubes.setdefault((c, second), []).append((first, device))
                     lattices.setdefault((c, first), []).append((second, device))
     return [[[n for _, n in sorted(g)] for g in groups.values()] for groups in (cubes, lattices)]
@@ -73,9 +74,9 @@
                 ) * jnp.float32(scale)
                 sums = sums.reshape(Y, C, ROWS, width)
                 for c, ref in enumerate((zero_ref, one_ref)):
-                    xc, zc = (x + X - c) % X, (z - c) % Z
+                    xc, zc = (x + X - START[c][0]) % X, (z - START[c][2]) % Z
                     for y in range(Y):
-                        ref[order(xc, (y - c) % Y, zc)] = sums[y, c]
+                        ref[order(xc, (y - START[c][1]) % Y, zc)] = sums[y, c]
             return carry
 
         lax.fori_loop(0, X, step, 0, unroll=True)

time: 72.7 us -> 71.9 us (0.989)
  the two profiles are of different devices: /device:TPU:2 before, /device:TPU:16 now
where the time goes in v6:
time: 71.9 us; the launch traced here: 71.6 us
  blocking collectives  62.1 us (86%)
  waiting for transfers between devices  4.13 us (6%)
  Pallas kernels  2.39 us (3%)
  starting transfers between devices  1.92 us (3%)
  other arithmetic  1.04 us (1%)
    all_to_all x2, blocking collectives, local(): lax.all_to_all(held, 'd', split_axis=0, concat_axis=0, axis_index_groups=...  62.1 us
    ppermute x1, waiting for transfers between devices, local(): other = lax.ppermute(send, 'd', [(i, i ^ 1) for i in range(ALL)])  4.13 us
    pallas_call x1, Pallas kernels, local(): pl.pallas_call(products, out_shape=[jax.ShapeDtypeStruct((8, ALL // C //...  2.39 us
    ppermute x1, starting transfers between devices, local(): other = lax.ppermute(send, 'd', [(i, i ^ 1) for i in range(ALL)])  1.92 us
  transfers between devices with their start and end apart: 1, of which 1 were waited for; matrix products, arithmetic and copies ran while one was open for 0% of the time, Pallas kernels for 0%

profile of v6, /device:TPU:16, one launch (start us, length us, event | category | flops | bytes accessed | tf_op | source)
XLA Modules:
  0.0 71.6 jit_solution(1204673484362526842)
XLA Ops:
  0.0 2.4 %products.1 = (f32[8,64,8,128]{3,2,1,0:T(8,128)S(1)}, f32[8,64,8,128]{3,2,1,0:T(8,128)S(1)}) custom-call(s32[2,32]{1,0:T(2,128)} %kept_any.1, s32[1,128]{1,0:T(1,128)} %bitcast.5, bf16[128,256]{1,0:T(8,128)(2,1)} %grad_any.1, bf16[128,8192]{1,0:T(8,128)(2,1)} %act_any.1), custom_call_target="tpu_custom_call" | custom-call | tf_op jit(solution)/shard_map/products/pallas_call | solution.py:92
  2.4 1.9 %collective-permute-start = (f32[8,64,8,128]{3,2,1,0:T(8,128)S(1)}, f32[8,64,8,128]{3,2,1,0:T(8,128)S(1)}, u32[]{:S(2)}, u32[]{:S(2)}) collective-permute-start(f32[8,64,8,128]{3,2,1,0:T(8,128)S(1)} %get-tuple-element.8), channel_id=1, source_target_pairs={{0,1},{1,0},{2,3},{3,2},{4,5},{5,4},{6,7},{7,6},{8,9},{9,8},{10,11... | collective-permute-start | bytes 6291464 | tf_op jit(solution)/shard_map/ppermute | solution.py:110
  4.3 4.1 %collective-permute-done = f32[8,64,8,128]{3,2,1,0:T(8,128)S(1)} collective-permute-done((f32[8,64,8,128]{3,2,1,0:T(8,128)S(1)}, f32[8,64,8,128]{3,2,1,0:T(8,128)S(1)}, u32[]{:S(2)}, u32[]{:S(2)}) %collective-permute-start) | collective-permute-done | bytes 2097184 | tf_op jit(solution)/shard_map/ppermute | solution.py:110
  8.5 0.3 add.3
  8.7 33.7 %all_to_all.10 = f32[512,8,128]{2,1,0:T(8,128)S(1)} all-to-all(f32[512,8,128]{2,1,0:T(8,128)S(1)} %bitcast.3), channel_id=1, replica_groups={{18,34,20,36,82,98,84,100},{514,50,516,52,578,114,580,116},{546,530,548..., dimensions={0} | all-to-all | bytes 4194304 | tf_op jit(solution)/shard_map/all_to_all | solution.py:113
  42.5 0.1 reduce_sum.18
  42.6 28.4 %all_to_all.11 = f32[64,8,128]{2,1,0:T(8,128)S(1)} all-to-all(f32[64,8,128]{2,1,0:T(8,128)S(1)} %reduce_sum.18), channel_id=1, replica_groups={{18,514,546,562,24,520,552,568,28,524,556,572,30,526,558,574,210,706,73..., dimensions={0} | all-to-all | bytes 524288 | tf_op jit(solution)/shard_map/all_to_all | solution.py:113
  71.0 0.7 reduce_sum.19
Async XLA Ops:
  2.4 6.1 %collective-permute-start = (f32[8,64,8,128]{3,2,1,0:T(8,128)S(1)}, f32[8,64,8,128]{3,2,1,0:T(8,128)S(1)}, u32[]{:S(2)}, u32[]{:S(2)}) collective-permute-start(f32[8,64,8,128]{3,2,1,0:T(8,128)S(1)} %get-tuple-element.8), channel_id=1, source_target_pairs={{0,1},{1,0},{2,3},{3,2},{4,5},{5,4},{6,7},{7,6},{8,9},{9,8},{10,11... | collective-permute-start | bytes 6291464 | tf_op jit(solution)/shard_map/ppermute | solution.py:110

commit v7 on v6

--- a/solution.py
+++ b/solution.py
@@ -12,7 +12,7 @@
 Z = ZH * ZL
 ALL = ZH * X * ZL * Y * C
 ROWS = 8
-START = ((0, 1, 1), (1, 0, 0))
+START = ((0, 1, 1), (1, 0, 4))
 
 
 def number(x, y, z, c):

time: 71.9 us -> 71.8 us (level)
  no operation moved by 1% of the time
where the time goes in v7:
time: 71.8 us; the launch traced here: 71.6 us
  blocking collectives  62.1 us (86%)
  waiting for transfers between devices  4.13 us (6%)
  Pallas kernels  2.39 us (3%)
  starting transfers between devices  1.92 us (3%)
  other arithmetic  1.04 us (1%)
    all_to_all x2, blocking collectives, local(): lax.all_to_all(held, 'd', split_axis=0, concat_axis=0, axis_index_groups=...  62.1 us
    ppermute x1, waiting for transfers between devices, local(): other = lax.ppermute(send, 'd', [(i, i ^ 1) for i in range(ALL)])  4.13 us
    pallas_call x1, Pallas kernels, local(): pl.pallas_call(products, out_shape=[jax.ShapeDtypeStruct((8, ALL // C //...  2.39 us
    ppermute x1, starting transfers between devices, local(): other = lax.ppermute(send, 'd', [(i, i ^ 1) for i in range(ALL)])  1.92 us
  transfers between devices with their start and end apart: 1, of which 1 were waited for; matrix products, arithmetic and copies ran while one was open for 0% of the time, Pallas kernels for 0%

profile of v7, /device:TPU:16, one launch (start us, length us, event | category | flops | bytes accessed | tf_op | source)
XLA Modules:
  0.0 71.6 jit_solution(8258149684407469012)
XLA Ops:
  0.0 2.4 %products.1 = (f32[8,64,8,128]{3,2,1,0:T(8,128)S(1)}, f32[8,64,8,128]{3,2,1,0:T(8,128)S(1)}) custom-call(s32[2,32]{1,0:T(2,128)} %kept_any.1, s32[1,128]{1,0:T(1,128)} %bitcast.5, bf16[128,256]{1,0:T(8,128)(2,1)} %grad_any.1, bf16[128,8192]{1,0:T(8,128)(2,1)} %act_any.1), custom_call_target="tpu_custom_call" | custom-call | tf_op jit(solution)/shard_map/products/pallas_call | solution.py:92
  2.4 1.9 %collective-permute-start = (f32[8,64,8,128]{3,2,1,0:T(8,128)S(1)}, f32[8,64,8,128]{3,2,1,0:T(8,128)S(1)}, u32[]{:S(2)}, u32[]{:S(2)}) collective-permute-start(f32[8,64,8,128]{3,2,1,0:T(8,128)S(1)} %get-tuple-element.8), channel_id=1, source_target_pairs={{0,1},{1,0},{2,3},{3,2},{4,5},{5,4},{6,7},{7,6},{8,9},{9,8},{10,11... | collective-permute-start | bytes 6291464 | tf_op jit(solution)/shard_map/ppermute | solution.py:110
  4.3 4.1 %collective-permute-done = f32[8,64,8,128]{3,2,1,0:T(8,128)S(1)} collective-permute-done((f32[8,64,8,128]{3,2,1,0:T(8,128)S(1)}, f32[8,64,8,128]{3,2,1,0:T(8,128)S(1)}, u32[]{:S(2)}, u32[]{:S(2)}) %collective-permute-start) | collective-permute-done | bytes 2097184 | tf_op jit(solution)/shard_map/ppermute | solution.py:110
  8.4 0.3 add.3
  8.7 33.7 %all_to_all.10 = f32[512,8,128]{2,1,0:T(8,128)S(1)} all-to-all(f32[512,8,128]{2,1,0:T(8,128)S(1)} %bitcast.3), channel_id=1, replica_groups={{18,34,20,36,82,98,84,100},{514,50,516,52,578,114,580,116},{546,530,548..., dimensions={0} | all-to-all | bytes 4194304 | tf_op jit(solution)/shard_map/all_to_all | solution.py:113
  42.5 0.1 reduce_sum.18
  42.6 28.3 %all_to_all.11 = f32[64,8,128]{2,1,0:T(8,128)S(1)} all-to-all(f32[64,8,128]{2,1,0:T(8,128)S(1)} %reduce_sum.18), channel_id=1, replica_groups={{18,514,546,562,24,520,552,568,28,524,556,572,30,526,558,574,210,706,73..., dimensions={0} | all-to-all | bytes 524288 | tf_op jit(solution)/shard_map/all_to_all | solution.py:113
  70.9 0.7 reduce_sum.19
Async XLA Ops:
  2.4 6.1 %collective-permute-start = (f32[8,64,8,128]{3,2,1,0:T(8,128)S(1)}, f32[8,64,8,128]{3,2,1,0:T(8,128)S(1)}, u32[]{:S(2)}, u32[]{:S(2)}) collective-permute-start(f32[8,64,8,128]{3,2,1,0:T(8,128)S(1)} %get-tuple-element.8), channel_id=1, source_target_pairs={{0,1},{1,0},{2,3},{3,2},{4,5},{5,4},{6,7},{7,6},{8,9},{9,8},{10,11... | collective-permute-start | bytes 6291464 | tf_op jit(solution)/shard_map/ppermute | solution.py:110
